TPU v7x, 32 devices: a whole 2x2x4 slice. The times are simulated.
32 devices in a mesh: section: 4 (over y, x), seq: 8 (over z, core).
Axes of the slice: x: 2, y: 2, z: 4, core: 2. Of those that a mesh axis runs over, the one named last changes fastest.
Arguments:
- features: bfloat16 [1024, 8192], P('seq', 'section'), may hold values from -600 to 600
- norm_gain: float32 [8192], P('section'), may hold values from 0.1 to 1.9
- kv_weight: bfloat16 [8192, 2048], P('section'), may hold values from -0.09375 to 0.09375
- queries: bfloat16 [3, 64, 1024, 128], P(None, 'section', 'seq'), may hold values from -64 to 64
- step_kv: bfloat16 [3, 8, 1024, 256], P(None, 'section', 'seq'), may hold values from -6 to 6
- doc_ids: int32 [1024], replicated, may hold values from 0 to 7, never falling along the last dimension, each value on 1 to 768 neighbouring positions
- block_lists: int32 [3, 16, 16], replicated, may hold values from 0 to 15, as said below
Outputs:
- attended: bfloat16 [3, 64, 1024, 128], P(None, 'section', 'seq')
- kv_cache: bfloat16 [8, 1024, 256], P('section', 'seq')
Inputs may be any that keep to these rules, and one draw needn't show every extreme that they name: `doc_ids`: document numbers never fall along the tokens; a document holds 1 to 768 tokens, and one holds exactly 768. `block_lists`: entry [k, b, 0] is b itself; every entry of row b is at most b; entries may repeat.
All inputs are finite; a program needn't handle non-finite values.
Results may differ from a plain program's by a relative error of at most 0.0084.
Values may be sent and summed in bfloat16 or wider, within the bound.
A program may use at most 128 MiB of HBM per device.

v0:
```python
import math

import jax
import jax.numpy as jnp
from jax import lax
from jax.sharding import PartitionSpec as P

neg_fill = -1e30


def row_marks(doc_ids, block_lists, anchor, amount, block_len, blocks):
    positions = anchor + jnp.arange(amount, dtype=jnp.int32)
    row_docs = lax.dynamic_slice_in_dim(doc_ids, anchor, amount, 0)
    row_lists = lax.dynamic_slice_in_dim(block_lists, anchor // block_len, amount // block_len, 1)
    row_table = jnp.any(row_lists[..., None] == jnp.arange(blocks, dtype=jnp.int32), axis=2)
    return (positions, row_docs, jnp.repeat(row_table, block_len, axis=1))


def per_device(features, norm_gain, kv_weight, queries, step_kv, doc_ids, block_lists):
    sections = lax.axis_size("section")
    own_shard = lax.axis_index("seq")
    step_total, local_heads, tok_dev, head_dim = queries.shape
    local_groups = step_kv.shape[1]
    group_size = local_heads // local_groups
    feature_width = features.shape[1] * sections
    blocks = block_lists.shape[1]
    block_len = doc_ids.shape[0] // blocks
    floated = features.astype(jnp.float32)
    squares = lax.psum(jnp.sum(floated * floated, axis=1), "section")
    inverse = lax.rsqrt(squares / feature_width + 1e-05)
    normalized = (floated * inverse[:, None] * norm_gain[None, :]).astype(jnp.bfloat16)
    all_groups = kv_weight.shape[1] // (2 * head_dim)
    weight_heads = kv_weight.reshape(kv_weight.shape[0], all_groups, 2 * head_dim)
    kv_cache = lax.psum_scatter(
        jnp.einsum("td,dgc->gtc", normalized, weight_heads, preferred_element_type=jnp.float32),
        "section",
        scatter_dimension=0,
        tiled=True,
    ).astype(jnp.bfloat16)
    own_first = own_shard * tok_dev
    positions, row_docs, row_table = row_marks(
        doc_ids, block_lists, own_first, tok_dev, block_len, blocks
    )
    row_total = queries.shape[2]
    grouped = queries.reshape(step_total, local_groups, group_size, row_total, head_dim)
    inv_sqrt = 1.0 / math.sqrt(head_dim)
    stat_shape = (step_total, local_groups, group_size, row_total)
    initial = (
        jnp.full(stat_shape, neg_fill, jnp.float32),
        jnp.zeros(stat_shape, jnp.float32),
        jnp.zeros(stat_shape + (head_dim,), jnp.float32),
    )
    incoming = lax.all_gather(kv_cache, "seq", axis=1, tiled=True)
    length = incoming.shape[1]
    key_pos = jnp.arange(length, dtype=jnp.int32)
    listed = row_table
    listed = jnp.repeat(listed, block_len, axis=2)
    allowed = (
        listed
        & (key_pos[None, :] <= positions[:, None])[None]
        & (doc_ids[None, :] == row_docs[:, None])[None]
    )

    def attend(running):
        run_max, run_sum, summed = running
        scores = (
            jnp.einsum(
                "skgrd,knd->skgrn",
                grouped,
                incoming[..., :head_dim],
                preferred_element_type=jnp.float32,
            )
            * inv_sqrt
        )
        visible = allowed[:, None, None]
        new_max = jnp.maximum(run_max, jnp.max(jnp.where(visible, scores, neg_fill), axis=-1))
        weights = jnp.where(visible, jnp.exp(scores - new_max[..., None]), 0.0)
        factor = jnp.exp(run_max - new_max)
        run_sum = jnp.sum(weights, axis=-1)
        summed = jnp.einsum(
            "skgrn,knd->skgrd",
            weights.astype(jnp.bfloat16),
            incoming[..., head_dim:],
            preferred_element_type=jnp.float32,
        )
        return (new_max, run_sum, summed)

    run_max, run_sum, summed = lax.cond(jnp.any(allowed), attend, lambda kept: kept, initial)
    step_index = jnp.arange(step_total, dtype=jnp.int32)
    own_mask = (step_index[None, :] <= step_index[:, None])[:, None, None, None, :]
    own_scores = (
        jnp.einsum(
            "skgrd,mkrd->skgrm",
            grouped,
            step_kv[..., :head_dim],
            preferred_element_type=jnp.float32,
        )
        * inv_sqrt
    )
    final_max = jnp.maximum(run_max, jnp.max(jnp.where(own_mask, own_scores, neg_fill), axis=-1))
    own_weights = jnp.where(own_mask, jnp.exp(own_scores - final_max[..., None]), 0.0)
    factor = jnp.exp(run_max - final_max)
    run_sum = run_sum * factor + jnp.sum(own_weights, axis=-1)
    summed = summed * factor[..., None] + jnp.einsum(
        "skgrm,mkrd->skgrd",
        own_weights.astype(jnp.bfloat16),
        step_kv[..., head_dim:],
        preferred_element_type=jnp.float32,
    )
    result = (
        (summed / run_sum[..., None])
        .astype(jnp.bfloat16)
        .reshape(step_total, local_heads, row_total, head_dim)
    )
    return (result, kv_cache)


def solution(mesh):
    in_specs = (
        P("seq", "section"),
        P("section"),
        P("section", None),
        P(None, "section", "seq", None),
        P(None, "section", "seq", None),
        P(),
        P(),
    )
    out_specs = (P(None, "section", "seq", None), P("section", "seq", None))
    return jax.shard_map(
        per_device, mesh=mesh, in_specs=in_specs, out_specs=out_specs, check_vma=False
    )
```

profile of v0, /device:TPU:0, one launch (start us, length us, event | category | flops | bytes accessed | tf_op | source)
XLA Modules:
  0.0 135.8 jit_solution(3898224606935802063)
XLA Ops:
  7.2 1.2 fusion.36
  8.5 11.4 %psum.7 = f32[128]{0:T(128)S(1)} all-reduce(f32[128]{0:T(128)S(1)} %fusion.36), channel_id=1, replica_groups=mesh['section'=4,'seq'=8] {'section'}, use_global_device_ids=true, to_apply=%region_3.4 | all-reduce | flops 128 | bytes 1024 | tf_op jit(solution)/shard_map/psum | solution.py:29
  19.8 6.0 %fusion.33 = f32[8,128,256]{2,1,0:T(8,128)} fusion(bf16[256,8,8,256]{3,2,1,0:T(8,128)(2,1)} %bitcast.86, bf16[128,2048]{1,0:T(8,128)(2,1)} %param.9, f32[2048]{0:T(1024)} %param.10, f32[128]{0:T(128)S(1)} %add_rsqrt_fusion), kind=kOutput, calls=%fused_computation.38 | convolution fusion | flops 1074790400 | bytes 9970176 | tf_op jit(solution)/shard_map/td,dgc->gtc/dot_general | solution.py:35
  25.9 27.2 %reduce-scatter.2.cloned.1.call-done = f32[2,128,256]{2,1,0:T(8,128)} async-done(((f32[8,128,256]{2,1,0:T(8,128)}), f32[2,128,256]{2,1,0:T(8,128)}) %reduce-scatter.2.cloned.1.call-update) | async-done | bytes 262160 | tf_op jit(solution)/shard_map/reduce_scatter | solution.py:34
  53.1 1.6 %convert_element_type.24 = bf16[2,128,256]{2,1,0:T(8,128)(2,1)} convert(f32[2,128,256]{2,1,0:T(8,128)} %reduce-scatter.2.cloned.1.call-done) | non-fusion elementwise | flops 65536 | bytes 393216 | tf_op jit(solution)/shard_map/convert_element_type | solution.py:39
  54.8 0.1 dynamic_slice.7
  54.9 0.1 fusion.49
  55.0 0.1 copy.57
  55.1 0.1 broadcast_in_dim.74
  55.2 0.1 reshape.116
  55.4 0.3 broadcast_compare_fusion.1
  55.7 1.0 and_reduce_fusion
  57.4 0.1 fusion.51
  57.5 6.3 %fusion.25 = (f32[3,2,8,128]{2,0,3,1:T(4,128)S(1)}, f32[2,128,3,3,8]{4,2,3,1,0:T(4,128)}) fusion(pred[3,3]{1,0:T(4,128)(4,1)S(1)} %iota_compare_fusion.1, bf16[3,2,8,128,128]{4,3,2,1,0:T(8,128)(2,1)S(1)} %bitcast.83, bf16[3,2,128,128]{3,2,1,0:T(8,128)(2,1)S(1)} %get-tuple-element.77), kind=kOutput, calls=%fused_computation.31 | convolution fusion | flops 4767744 | bytes 1867785 | tf_op jit(solution)/shard_map/skgrd,mkrd->skgrm/dot_general | solution.py:92
  63.8 0.1 copy.63
  64.0 13.5 %all-gather.2.cloned.1.call-done = bf16[2,1024,256]{2,1,0:T(8,128)(2,1)} async-done(((bf16[2,128,256]{2,1,0:T(8,128)(2,1)}), bf16[2,1024,256]{2,1,0:T(8,128)(2,1)}) %all-gather.2.cloned.1.call-update) | async-done | bytes 1048592 | tf_op jit(solution)/shard_map/all_gather | solution.py:53
  77.5 0.1 broadcast_in_dim.75
  77.6 37.2 %conditional.1 = (f32[3,2,8,128,128]{4,2,0,3,1:T(8,128)S(1)}, f32[3,2,8,128]{3,2,1,0:T(8,128)S(1)}, f32[3,2,8,128]{3,2,1,0:T(8,128)S(1)}) conditional(s32[]{:T(128)} %convert_element_type.21, () %tuple.16, (pred[3,128,16,64]{1,3,2,0:T(8,128)(4,1)S(1)}, s32[128]{0:T(128)S(1)}, s32[1,128,1024]{1,2,0:T(8,128)S(1)}, s32[1024]{0:T(1024)S(1)}, ...), branch_computations={%region_5.6_spmd, %region_6.9_spmd} | conditional | flops 3291473920 | bytes 95015992 | solution.py:88
  77.8 0.2 broadcast_compare_fusion
  78.1 0.1 compare_bitcast_fusion
  78.1 0.3 fusion.13
  78.5 11.2 %fusion = (f32[3,2,8,128]{3,2,0,1:T(8,128)S(1)}, f32[2,1024,3,8,128]{4,1,3,2,0:T(8,128)}) fusion(pred[3,128,1024]{1,2,0:T(8,128)(4,1)S(1)} %fusion.13, bf16[3,2,8,128,128]{4,3,2,1,0:T(8,128)(2,1)S(1)} %get-tuple-element.68, bf16[2,1024,256]{2,1,0:T(8,128)(2,1)} %get-tuple-element.31), kind=kOutput, calls=%fused_computation.2 | convolution fusion | flops 1629480960 | bytes 27680768 | tf_op jit(solution)/shard_map/cond/branch_1_fun/skgrd,knd->skgrn/dot_general | solution.py:67
  89.7 11.0 %fusion.4 = f32[3,2,8,128]{3,2,0,1:T(8,128)S(1)} fusion(f32[2,1024,3,8,128]{4,1,3,2,0:T(8,128)} %get-tuple-element.75, f32[3,2,8,128]{3,2,0,1:T(8,128)S(1)} %broadcast_maximum_fusion, pred[3,128,1024]{1,2,0:T(8,128)(4,1)S(1)} %fusion.13), kind=kLoop, calls=%fused_computation.6 | loop fusion | flops 25159680 | bytes 25608192 | tf_op jit(solution)/shard_map/cond/branch_1_fun/reduce_sum | solution.py:79
  100.7 12.1 %fusion.8 = f32[3,2,8,128,128]{4,3,2,0,1:T(8,128)S(1)} fusion(f32[2,1024,3,8,128]{4,1,3,2,0:T(8,128)} %get-tuple-element.75, f32[3,2,8,128]{3,2,0,1:T(8,128)S(1)} %broadcast_maximum_fusion, pred[3,128,1024]{1,2,0:T(8,128)(4,1)S(1)} %fusion.13, bf16[2,1024,256]{2,1,0:T(8,128)(2,1)S(1)} %copy-done.3), kind=kOutput, calls=%fused_computation.9 | convolution fusion | flops 1635778560 | bytes 29253632 | tf_op jit(solution)/shard_map/cond/branch_1_fun/skgrn,knd->skgrd/dot_general | solution.py:80
  112.8 1.8 %copy.79 = f32[3,2,8,128,128]{4,2,0,3,1:T(8,128)S(1)} copy(f32[3,2,8,128,128]{4,3,2,0,1:T(8,128)S(1)} %fusion.8) | data formatting | bytes 6291456 | tf_op jit(solution)/shard_map/cond | solution.py:88
  114.9 1.0 copy.67
  115.9 3.9 %fusion.39 = f32[3,2,8,128]{2,0,3,1:T(4,128)} fusion(f32[2,128,3,3,8]{4,2,3,1,0:T(4,128)} %get-tuple-element.79, f32[3,2,8,128]{2,0,3,1:T(4,128)} %copy.67, pred[3,3]{1,0:T(4,128)(4,1)S(1)} %iota_compare_fusion.1), kind=kLoop, calls=%fused_computation.44 | loop fusion | flops 49152 | bytes 122889 | tf_op jit(solution)/shard_map/reduce_sum | solution.py:103
  119.8 1.2 copy.70
  121.0 1.0 copy.71
  122.0 1.0 copy.65
  123.0 4.4 %fusion.24 = bf16[3,2,8,128,128]{4,2,0,3,1:T(8,128)(2,1)S(1)} fusion(f32[3,2,8,128,128]{4,2,0,3,1:T(8,128)S(1)} %get-tuple-element.69, f32[3,2,8,128]{2,0,3,1:T(4,128)} %copy.71, f32[3,2,8,128]{2,0,3,1:T(4,128)} %copy.65, f32[2,128,3,3,8]{4,2,3,1,0:T(4,128)} %get-tuple-element.79, f32[3,2,8,128]{2,0,3,1:T(4,128)} %copy.67, ...), kind=kOutput, calls=%fused_computation.28 | convolution fusion | flops 7919616 | bytes 5062665 | tf_op jit(solution)/shard_map/skgrm,mkrd->skgrd/dot_general | solution.py:104
  127.5 1.5 %copy.72 = bf16[3,2,8,128,128]{4,3,2,1,0:T(8,128)(2,1)} copy(bf16[3,2,8,128,128]{4,2,0,3,1:T(8,128)(2,1)S(1)} %fusion.24) | data formatting | bytes 3145728 | tf_op jit(solution)/shard_map/convert_element_type | solution.py:112
  (26 shorter events, 0.3 us)
Async XLA Ops:
  7.2 47.7 %copy-start = (s32[3,16,16]{2,1,0:T(8,128)S(1)}, s32[3,16,16]{2,1,0:T(8,128)}, u32[]{:S(2)}) copy-start(s32[3,16,16]{2,1,0:T(8,128)} %param.15) | copy-start | bytes 9220
  7.2 45.9 %reduce-scatter.2.cloned.1.call-start = ((), (), s32[]{:S(2)}) async-start(), calls=%async_computation.1 | async-start | bytes 1310720 | tf_op jit(solution)/shard_map/reduce_scatter | solution.py:34
  19.8 34.9 %copy-start.4 = (s32[1024]{0:T(1024)S(1)}, s32[1024]{0:T(1024)}, u32[]{:S(2)}) copy-start(s32[1024]{0:T(1024)} %param.14) | copy-start | bytes 12292
  19.8 37.6 %copy-start.2 = (bf16[3,2,128,256]{3,2,1,0:T(8,128)(2,1)S(1)}, bf16[3,2,128,256]{3,2,1,0:T(8,128)(2,1)}, u32[]{:S(2)}) copy-start(bf16[3,2,128,256]{3,2,1,0:T(8,128)(2,1)} %param.13) | copy-start | bytes 1179652
  19.8 37.7 %copy-start.1 = (bf16[3,16,128,128]{3,2,1,0:T(8,128)(2,1)S(1)}, bf16[3,16,128,128]{3,2,1,0:T(8,128)(2,1)}, u32[]{:S(2)}) copy-start(bf16[3,16,128,128]{3,2,1,0:T(8,128)(2,1)} %param.12) | copy-start | bytes 4718596
  25.8 51.6 %all-gather.2.cloned.1.call-start = ((), (), s32[]{:S(2)}) async-start(), calls=%async_computation.2 | async-start | bytes 1179648 | tf_op jit(solution)/shard_map/all_gather | solution.py:53
  89.7 11.0 %copy-start.3 = (bf16[2,1024,256]{2,1,0:T(8,128)(2,1)S(1)}, bf16[2,1024,256]{2,1,0:T(8,128)(2,1)}, u32[]{:S(2)}) copy-start(bf16[2,1024,256]{2,1,0:T(8,128)(2,1)} %get-tuple-element.31) | copy-start | bytes 3145732 | tf_op jit(solution)/shard_map/cond
Sparse Core Ops, SparseCore 0:
  26.0 27.0 reduce-scatter.1
  55.3 22.0 all-gather.1
where the time goes:
time: 136 us
  waiting for transfers between devices  40.7 us (30%)
  matrix products  40 us (29%)
  other arithmetic  19.9 us (15%)
  between operations  14.9 us (11%)
  blocking collectives  11.4 us (8%)
  local copies, waits for them, and re-layouts  8.44 us (6%)
    reduce_scatter x1, waiting for transfers between devices, per_device(): lax.psum_scatter(jnp.einsum('td,dgc->gtc', normalized, weight_heads, pref...  27.2 us
    all_gather x1, waiting for transfers between devices, per_device(): incoming = lax.all_gather(kv_cache, 'seq', axis=1, tiled=True)  13.5 us
    dot_general x1, matrix products, attend(): jnp.einsum('skgrn,knd->skgrd', weights.astype(jnp.bfloat16), incoming[......  12.1 us
    psum x1, blocking collectives, per_device(): squares = lax.psum(jnp.sum(floated * floated, axis=1), 'section')  11.4 us
    dot_general x1, matrix products, attend(): jnp.einsum('skgrd,knd->skgrn', grouped, incoming[..., :head_dim], preferr...  11.2 us
    reduce_sum x1, other arithmetic, attend(): run_sum = jnp.sum(weights, axis=-1)  11 us
    dot_general x1, matrix products, per_device(): jnp.einsum('skgrd,mkrd->skgrm', grouped, step_kv[..., :head_dim], preferr...  6.3 us
    dot_general x1, matrix products, per_device(): jnp.einsum('td,dgc->gtc', normalized, weight_heads, preferred_element_typ...  5.98 us
  transfers between devices with their start and end apart: 2, of which 2 were waited for; matrix products, arithmetic and copies ran while one was open for 6% of the time, Pallas kernels for 0%

commit v1 on v0

v1 whole, which is shorter than its diff:
```python
import functools
import math

import jax
import jax.numpy as jnp
from jax import lax
from jax.experimental import pallas as pl
from jax.experimental.pallas import tpu as pltpu
from jax.sharding import PartitionSpec as P

neg_fill = -1e30
MESH = pl.DeviceIdType.MESH
CORES = 2


def flipped(index, mask, count):
    result, bit = 0, 1
    while bit < count:
        own = (index // bit) % 2
        result = result + bit * ((1 - own) if mask & bit else own)
        bit *= 2
    return result


def kv_kernel(
    sections, shards, feature_width,
    feat_ref, gain_ref, weight_ref, kv_ref,
    weight_buf, scaled, own_part, send_buf, recv_buf, square_send, square_recv,
    weight_sem, rs_send, rs_recv, sq_send, sq_recv, chain_send, chain_recv, twin_send, twin_recv,
):
    section = lax.axis_index("section")
    shard = lax.axis_index("seq")
    groups, _, tokens, width = kv_ref.shape
    pairs = shards // CORES
    pair, core = shard // CORES, shard % CORES
    twin = pair * CORES + 1 - core
    later, earlier = shard + CORES, shard - CORES
    order = [(g, k) for g in range(groups) for k in range(sections - 1, -1, -1)]

    def weight_copy(slot):
        g, k = order[slot]
        column = pl.multiple_of((flipped(section, k, sections) * groups + g) * width, width)
        return pltpu.make_async_copy(
            weight_ref.at[:, pl.ds(column, width)], weight_buf.at[slot], weight_sem.at[slot]
        )

    for slot in range(len(order)):
        weight_copy(slot).start()

    barrier = pltpu.get_barrier_semaphore()
    for k in range(1, sections):
        pl.semaphore_signal(
            barrier, inc=1, device_id={"section": flipped(section, k, sections)}, device_id_type=MESH
        )
    pl.semaphore_signal(barrier, inc=1, device_id={"seq": twin}, device_id_type=MESH)

    @pl.when(pair < pairs - 1)
    def _():
        pl.semaphore_signal(barrier, inc=1, device_id={"seq": later}, device_id_type=MESH)

    @pl.when(pair > 0)
    def _():
        pl.semaphore_signal(barrier, inc=1, device_id={"seq": earlier}, device_id_type=MESH)

    floated = feat_ref[...].astype(jnp.float32)
    scaled[...] = (floated * gain_ref[...]).astype(jnp.bfloat16)
    squares = jnp.sum(floated * floated, axis=1, keepdims=True)
    square_rows = jnp.transpose(jnp.broadcast_to(squares, (tokens, tokens)))[:8]
    square_send[...] = square_rows

    pl.semaphore_wait(barrier, sections + jnp.where(pair > 0, 1, 0) + jnp.where(pair < pairs - 1, 1, 0))

    def square_copy(k):
        return pltpu.make_async_remote_copy(
            src_ref=square_send, dst_ref=square_recv.at[k - 1],
            send_sem=sq_send.at[k - 1], recv_sem=sq_recv.at[k - 1],
            device_id={"section": flipped(section, k, sections)}, device_id_type=MESH,
        )

    def part_copy(g, k):
        return pltpu.make_async_remote_copy(
            src_ref=send_buf.at[g, k - 1], dst_ref=recv_buf.at[g, k - 1],
            send_sem=rs_send.at[g, k - 1], recv_sem=rs_recv.at[g, k - 1],
            device_id={"section": flipped(section, k, sections)}, device_id_type=MESH,
        )

    def chain_copy(g, hop):
        place = kv_ref.at[g, shard - CORES * hop]
        return pltpu.make_async_remote_copy(
            src_ref=place, dst_ref=place,
            send_sem=chain_send.at[g, hop], recv_sem=chain_recv.at[g, hop],
            device_id={"seq": later}, device_id_type=MESH,
        )

    def twin_copy(g, hop):
        place = kv_ref.at[g, shard - CORES * hop]
        return pltpu.make_async_remote_copy(
            src_ref=place, dst_ref=place,
            send_sem=twin_send.at[g, hop], recv_sem=twin_recv.at[g, hop],
            device_id={"seq": twin}, device_id_type=MESH,
        )

    def chain_arrival(g, hop):
        place = kv_ref.at[g, shard - CORES * hop]
        return pltpu.make_async_remote_copy(
            src_ref=place, dst_ref=place,
            send_sem=chain_send.at[g, hop - 1], recv_sem=chain_recv.at[g, hop - 1],
            device_id={"seq": later}, device_id_type=MESH,
        )

    def twin_arrival(g, hop):
        place = kv_ref.at[g, twin - CORES * hop]
        return pltpu.make_async_remote_copy(
            src_ref=place, dst_ref=place,
            send_sem=twin_send.at[g, hop], recv_sem=twin_recv.at[g, hop],
            device_id={"seq": twin}, device_id_type=MESH,
        )

    for k in range(1, sections):
        square_copy(k).start()

    for slot, (g, k) in enumerate(order):
        weight_copy(slot).wait()
        part = jnp.dot(scaled[...], weight_buf[slot], preferred_element_type=jnp.float32)
        if k:
            send_buf[g, k - 1] = part.astype(jnp.bfloat16)
            part_copy(g, k).start()
        else:
            own_part[g] = part

    total = square_rows
    for k in range(1, sections):
        square_copy(k).wait()
        total = total + square_recv[k - 1]
    mean = jnp.transpose(jnp.broadcast_to(total[:1], (tokens, tokens))) / feature_width
    inverse = jnp.concatenate([lax.rsqrt(mean + 1e-05)] * (width // tokens), axis=1)

    for g in range(groups):
        summed = own_part[g]
        for k in range(sections - 1, 0, -1):
            part_copy(g, k).wait_recv()
            summed = summed + recv_buf[g, k - 1].astype(jnp.float32)
        kv_ref[g, shard] = (summed * inverse).astype(jnp.bfloat16)

        @pl.when(pair < pairs - 1)
        def _():
            chain_copy(g, 0).start()

        twin_copy(g, 0).start()

    for hop in range(1, pairs):
        @pl.when(hop <= pair)
        def _():
            for g in range(groups):
                chain_arrival(g, hop).wait_recv()

                @pl.when(pair < pairs - 1)
                def _():
                    chain_copy(g, hop).start()

                twin_copy(g, hop).start()

    for hop in range(pairs):
        @pl.when(hop <= pair)
        def _():
            for g in range(groups):
                twin_arrival(g, hop).wait_recv()
                twin_copy(g, hop).wait_send()

                @pl.when(pair < pairs - 1)
                def _():
                    chain_copy(g, hop).wait_send()

    for g in range(groups):
        for k in range(1, sections):
            part_copy(g, k).wait_send()


def attend_kernel(
    block_len, entries,
    doc_smem, list_smem, docs_ref, query_ref, step_ref, kv_ref, out_ref, cache_ref,
    bias, step_scores, scores, top, total, acc,
):
    shard = lax.axis_index("seq")
    step = pl.program_id(1)
    _, heads, tokens, head_dim = query_ref.shape
    steps = step_ref.shape[0]
    shards = kv_ref.shape[1]
    chunk = CORES * tokens
    chunks = shards // CORES
    pair = shard // CORES
    scale = math.log2(math.e) / math.sqrt(head_dim)
    contract_last = (((1,), (1,)), ((), ()))

    cache_ref[0] = kv_ref[0, shard]

    first_doc = doc_smem[shard * tokens]
    lowest = jnp.int32(0)
    for c in range(chunks):
        lowest = lowest + jnp.where(doc_smem[c * chunk + chunk - 1] < first_doc, 1, 0)

    row = lax.broadcasted_iota(jnp.int32, (tokens, tokens), 0)
    column = lax.broadcasted_iota(jnp.int32, (tokens, tokens), 1)
    lane = lax.broadcasted_iota(jnp.int32, (1, tokens), 1)
    diagonal = jnp.where(row == column, 0.0, neg_fill)
    own_docs = docs_ref[pl.ds(shard, 1), :].astype(jnp.float32)
    row_docs = jnp.transpose(jnp.broadcast_to(own_docs, (tokens, tokens)))
    row_blocks = tokens // block_len

    def score(queries, keys):
        return lax.dot_general(queries, keys, contract_last, preferred_element_type=jnp.float32)

    for h in range(heads):
        first = score(query_ref[0, h], step_ref[0, 0, :, :head_dim]) + diagonal
        step_scores[0, h] = first
        top[h] = first
    for m in range(1, steps):
        @pl.when(m <= step)
        def _():
            for h in range(heads):
                more = score(query_ref[0, h], step_ref[m, 0, :, :head_dim]) + diagonal
                step_scores[m, h] = more
                top[h] = jnp.maximum(top[h], more)

    def first_pass(c, _):
        halves = []
        for half in range(CORES):
            key_shard = c * CORES + half
            key_block = key_shard * row_blocks + lane // block_len
            listed = []
            for r in range(row_blocks):
                marks = jnp.full((1, tokens), neg_fill, jnp.float32)
                for e in range(entries):
                    entry = list_smem[(step * shards + shard) * row_blocks * entries + r * entries + e]
                    marks = jnp.where(key_block == entry, 0.0, marks)
                listed.append(marks)
            marks = jnp.broadcast_to(listed[-1], (tokens, tokens))
            for r in range(row_blocks - 2, -1, -1):
                marks = jnp.where(row < (r + 1) * block_len, listed[r], marks)
            key_docs = docs_ref[pl.ds(key_shard, 1), :].astype(jnp.float32)
            marks = jnp.where(row_docs == key_docs, marks, neg_fill)
            marks = jnp.where(key_shard * tokens + column <= shard * tokens + row, marks, neg_fill)
            halves.append(marks)
        bias[...] = jnp.concatenate(halves, axis=1)
        keys = kv_ref[0, pl.ds(c * CORES, CORES), :, :head_dim].reshape(chunk, head_dim)
        for h in range(heads):
            found = score(query_ref[0, h], keys) + bias[...]
            scores[c, h] = found
            top[h] = jnp.maximum(top[h], jnp.maximum(found[:, :tokens], found[:, tokens:]))
        return 0

    lax.fori_loop(lowest, pair + 1, first_pass, 0)

    for h in range(heads):
        highest = jnp.max(top[h], axis=1, keepdims=True) * scale
        top[h] = jnp.broadcast_to(highest, (tokens, tokens))

    for h in range(heads):
        weight = jnp.exp2(step_scores[0, h] * scale - top[h])
        total[h] = weight
        acc[h] = jnp.dot(
            weight.astype(jnp.bfloat16), step_ref[0, 0, :, head_dim:], preferred_element_type=jnp.float32
        )
    for m in range(1, steps):
        @pl.when(m <= step)
        def _():
            for h in range(heads):
                weight = jnp.exp2(step_scores[m, h] * scale - top[h])
                total[h] += weight
                acc[h] += jnp.dot(
                    weight.astype(jnp.bfloat16), step_ref[m, 0, :, head_dim:],
                    preferred_element_type=jnp.float32,
                )

    def second_pass(c, _):
        values = kv_ref[0, pl.ds(c * CORES, CORES), :, head_dim:].reshape(chunk, head_dim)
        for h in range(heads):
            highest = jnp.concatenate([top[h]] * CORES, axis=1)
            weight = jnp.exp2(scores[c, h] * scale - highest)
            total[h] += weight[:, :tokens] + weight[:, tokens:]
            acc[h] += jnp.dot(weight.astype(jnp.bfloat16), values, preferred_element_type=jnp.float32)
        return 0

    lax.fori_loop(lowest, pair + 1, second_pass, 0)

    for h in range(heads):
        denominator = jnp.sum(total[h], axis=1, keepdims=True)
        out_ref[0, h] = (acc[h] / denominator).astype(out_ref.dtype)


def per_device(sections, shards, features, norm_gain, kv_weight, queries, step_kv, doc_ids, block_lists):
    steps, local_heads, tokens, head_dim = queries.shape
    groups = step_kv.shape[1]
    group_size = local_heads // groups
    width = 2 * head_dim
    local_width = features.shape[1]
    blocks, entries = block_lists.shape[1:]
    block_len = doc_ids.shape[0] // blocks
    pairs = shards // CORES
    others = sections - 1
    dma = pltpu.SemaphoreType.DMA
    vmem = pl.BlockSpec(memory_space=pltpu.VMEM)

    kv_all = pl.pallas_call(
        functools.partial(kv_kernel, sections, shards, local_width * sections),
        out_shape=jax.ShapeDtypeStruct((groups, shards, tokens, width), jnp.bfloat16),
        in_specs=[vmem, vmem, pl.BlockSpec(memory_space=pl.ANY)],
        out_specs=vmem,
        scratch_shapes=[
            pltpu.VMEM((groups * sections, local_width, width), jnp.bfloat16),
            pltpu.VMEM((tokens, local_width), jnp.bfloat16),
            pltpu.VMEM((groups, tokens, width), jnp.float32),
            pltpu.VMEM((groups, others, tokens, width), jnp.bfloat16),
            pltpu.VMEM((groups, others, tokens, width), jnp.bfloat16),
            pltpu.VMEM((8, tokens), jnp.float32),
            pltpu.VMEM((others, 8, tokens), jnp.float32),
            dma((groups * sections,)),
            dma((groups, others)),
            dma((groups, others)),
            dma((others,)),
            dma((others,)),
            dma((groups, pairs)),
            dma((groups, pairs)),
            dma((groups, pairs)),
            dma((groups, pairs)),
        ],
        compiler_params=pltpu.CompilerParams(
            collective_id=0, has_side_effects=True, vmem_limit_bytes=32 * 1024 * 1024
        ),
    )(features, norm_gain.reshape(1, local_width), kv_weight)

    smem = pl.BlockSpec(memory_space=pltpu.SMEM)
    square = pltpu.VMEM((group_size, tokens, tokens), jnp.float32)
    attended, kv_cache = pl.pallas_call(
        functools.partial(attend_kernel, block_len, entries),
        grid=(groups, steps),
        out_shape=(
            jax.ShapeDtypeStruct(queries.shape, jnp.bfloat16),
            jax.ShapeDtypeStruct((groups, tokens, width), jnp.bfloat16),
        ),
        in_specs=[
            smem,
            smem,
            vmem,
            pl.BlockSpec((1, group_size, tokens, head_dim), lambda g, s: (s, g, 0, 0)),
            pl.BlockSpec((steps, 1, tokens, width), lambda g, s: (0, g, 0, 0)),
            pl.BlockSpec((1, shards, tokens, width), lambda g, s: (g, 0, 0, 0)),
        ],
        out_specs=(
            pl.BlockSpec((1, group_size, tokens, head_dim), lambda g, s: (s, g, 0, 0)),
            pl.BlockSpec((1, tokens, width), lambda g, s: (g, 0, 0)),
        ),
        scratch_shapes=[
            pltpu.VMEM((tokens, CORES * tokens), jnp.float32),
            pltpu.VMEM((steps, group_size, tokens, tokens), jnp.float32),
            pltpu.VMEM((pairs, group_size, tokens, CORES * tokens), jnp.float32),
            square,
            square,
            pltpu.VMEM((group_size, tokens, head_dim), jnp.float32),
        ],
        compiler_params=pltpu.CompilerParams(vmem_limit_bytes=48 * 1024 * 1024),
    )(
        doc_ids,
        block_lists.reshape(-1),
        doc_ids.reshape(shards, tokens),
        queries,
        step_kv,
        kv_all,
    )
    return (attended, kv_cache)


def solution(mesh):
    in_specs = (
        P("seq", "section"),
        P("section"),
        P("section", None),
        P(None, "section", "seq", None),
        P(None, "section", "seq", None),
        P(),
        P(),
    )
    out_specs = (P(None, "section", "seq", None), P("section", "seq", None))
    body = functools.partial(per_device, mesh.shape["section"], mesh.shape["seq"])
    return jax.shard_map(body, mesh=mesh, in_specs=in_specs, out_specs=out_specs, check_vma=False)
```

time: 136 us -> 53.2 us (0.39)
  the two profiles are of different devices: /device:TPU:0 before, /device:TPU:24 now
where the time goes in v1:
time: 53.2 us; the launch traced here: 52.4 us
  Pallas kernels  45.8 us (86%)
  local copies, waits for them, and re-layouts  5.94 us (11%)
  between operations  0.67 us (1%)
    pallas_call x1, Pallas kernels, per_device(): pl.pallas_call(functools.partial(attend_kernel, block_len, entries), grid...  24.9 us
    pallas_call x1, Pallas kernels, per_device(): pl.pallas_call(functools.partial(kv_kernel, sections, shards, local_width...  20.9 us
    unnamed x12, local copies, waits for them, and re-layouts  5.13 us

profile of v1, /device:TPU:24, one launch (start us, length us, event | category | flops | bytes accessed | tf_op | source)
XLA Modules:
  0.0 52.4 jit_solution(13078304138322417236)
XLA Ops:
  0.6 0.8 %reshape.13.list_smem = s32[768]{0:T(1024)S(1)} reshape(s32[3,16,16]{2,1,0:T(8,128)} %param.13) | data formatting | bytes 6144 | tf_op jit(solution)/shard_map/reshape | solution.py:364
  1.4 0.0 copy-start
  1.4 3.4 %copy-done = bf16[2048,2048]{1,0:T(8,128)(2,1)S(1)} copy-done((bf16[2048,2048]{1,0:T(8,128)(2,1)S(1)}, bf16[2048,2048]{1,0:T(8,128)(2,1)}, u32[]{:S(2)}) %copy-start) | copy-done | bytes 8388632
  4.8 0.0 copy-start.2
  4.8 1.0 %copy-done.2 = bf16[128,2048]{1,0:T(8,128)(2,1)S(1)} copy-done((bf16[128,2048]{1,0:T(8,128)(2,1)S(1)}, bf16[128,2048]{1,0:T(8,128)(2,1)}, u32[]{:S(2)}) %copy-start.2) | copy-done | bytes 524312
  5.9 0.0 copy-start.5
  5.9 0.7 %copy-done.5 = f32[2048]{0:T(1024)S(1)} copy-done((f32[2048]{0:T(1024)S(1)}, f32[2048]{0:T(1024)}, u32[]{:S(2)}) %copy-start.5) | copy-done | bytes 8216
  6.6 0.0 copy-start.1
  6.6 0.0 copy-start.3
  6.6 0.0 copy-start.4
  6.6 20.9 %shard_map.86.kv_ref = bf16[2,8,128,256]{3,2,1,0:T(8,128)(2,1)S(1)} custom-call(bf16[128,2048]{1,0:T(8,128)(2,1)S(1)} %copy-done.2, f32[1,2048]{1,0:T(1,128)S(1)} %bitcast.3, bf16[2048,2048]{1,0:T(8,128)(2,1)S(1)} %copy-done), custom_call_target="tpu_custom_call" | custom-call | tf_op jit(solution)/shard_map/pallas_call | solution.py:304
  27.5 0.0 copy-done.1
  27.5 0.0 copy-done.3
  27.5 0.0 copy-done.4
  27.5 24.9 %shard_map.87 = (bf16[3,16,128,128]{3,2,1,0:T(8,128)(2,1)}, bf16[2,128,256]{2,1,0:T(8,128)(2,1)}) custom-call(s32[1024]{0:T(1024)S(1)} %copy-done.4, s32[768]{0:T(1024)S(1)} %reshape.13.list_smem, s32[8,128]{1,0:T(8,128)S(1)} %bitcast.2, bf16[3,16,128,128]{3,2,1,0:T(8,128)(2,1)S(1)} %copy-done.1, bf16[3,2,128,256]{3,2,1,0:T(8,128)(2,1)S(1)} %copy-done.3, ...), custom_call_target="tpu_custom_call" | custom-call | tf_op jit(solution)/shard_map/pallas_call | solution.py:334
Async XLA Ops:
  1.4 3.4 %copy-start = (bf16[2048,2048]{1,0:T(8,128)(2,1)S(1)}, bf16[2048,2048]{1,0:T(8,128)(2,1)}, u32[]{:S(2)}) copy-start(bf16[2048,2048]{1,0:T(8,128)(2,1)} %weight_ref.1) | copy-start | bytes 25165828
  4.8 1.0 %copy-start.2 = (bf16[128,2048]{1,0:T(8,128)(2,1)S(1)}, bf16[128,2048]{1,0:T(8,128)(2,1)}, u32[]{:S(2)}) copy-start(bf16[128,2048]{1,0:T(8,128)(2,1)} %feat_ref.1) | copy-start | bytes 1572868
  5.9 0.7 %copy-start.5 = (f32[2048]{0:T(1024)S(1)}, f32[2048]{0:T(1024)}, u32[]{:S(2)}) copy-start(f32[2048]{0:T(1024)} %param.8) | copy-start | bytes 24580
  6.6 20.9 %copy-start.1 = (bf16[3,16,128,128]{3,2,1,0:T(8,128)(2,1)S(1)}, bf16[3,16,128,128]{3,2,1,0:T(8,128)(2,1)}, u32[]{:S(2)}) copy-start(bf16[3,16,128,128]{3,2,1,0:T(8,128)(2,1)} %query_ref.1) | copy-start | bytes 4718596
  6.6 20.9 %copy-start.3 = (bf16[3,2,128,256]{3,2,1,0:T(8,128)(2,1)S(1)}, bf16[3,2,128,256]{3,2,1,0:T(8,128)(2,1)}, u32[]{:S(2)}) copy-start(bf16[3,2,128,256]{3,2,1,0:T(8,128)(2,1)} %step_ref.1) | copy-start | bytes 1179652
  6.6 20.9 %copy-start.4 = (s32[1024]{0:T(1024)S(1)}, s32[1024]{0:T(1024)}, u32[]{:S(2)}) copy-start(s32[1024]{0:T(1024)} %doc_smem.1) | copy-start | bytes 12292

commit v2 on v1

v2 whole, which is shorter than its diff:
```python
import functools
import math

import jax
import jax.numpy as jnp
from jax import lax
from jax.experimental import pallas as pl
from jax.experimental.pallas import tpu as pltpu
from jax.sharding import PartitionSpec as P

neg_fill = -1e30
MESH = pl.DeviceIdType.MESH
CORES = 2


def flipped(index, mask, count):
    result, bit = 0, 1
    while bit < count:
        own = (index // bit) % 2
        result = result + bit * ((1 - own) if mask & bit else own)
        bit *= 2
    return result


def kv_kernel(
    sections, shards, feature_width,
    feat_ref, gain_ref, weight_ref, kv_ref,
    features, gain, weight_buf, scaled, own_part, send_buf, recv_buf, square_send, square_recv,
    load_sem, weight_sem, rs_send, rs_recv, sq_send, sq_recv, chain_send, chain_recv, twin_send, twin_recv,
):
    section = lax.axis_index("section")
    shard = lax.axis_index("seq")
    groups, _, tokens, width = kv_ref.shape
    pairs = shards // CORES
    pair, core = shard // CORES, shard % CORES
    twin = pair * CORES + 1 - core
    later, earlier = shard + CORES, shard - CORES
    order = [(g, k) for g in range(groups) for k in range(sections - 1, -1, -1)]

    def weight_copy(slot):
        g, k = order[slot]
        column = pl.multiple_of((flipped(section, k, sections) * groups + g) * width, width)
        return pltpu.make_async_copy(
            weight_ref.at[:, pl.ds(column, width)], weight_buf.at[slot], weight_sem.at[slot]
        )

    feature_load = pltpu.make_async_copy(feat_ref, features, load_sem.at[0])
    gain_load = pltpu.make_async_copy(gain_ref, gain, load_sem.at[1])
    feature_load.start()
    gain_load.start()
    for slot in range(len(order)):
        weight_copy(slot).start()

    barrier = pltpu.get_barrier_semaphore()
    for k in range(1, sections):
        pl.semaphore_signal(
            barrier, inc=1, device_id={"section": flipped(section, k, sections)}, device_id_type=MESH
        )
    pl.semaphore_signal(barrier, inc=1, device_id={"seq": twin}, device_id_type=MESH)

    @pl.when(pair < pairs - 1)
    def _():
        pl.semaphore_signal(barrier, inc=1, device_id={"seq": later}, device_id_type=MESH)

    @pl.when(pair > 0)
    def _():
        pl.semaphore_signal(barrier, inc=1, device_id={"seq": earlier}, device_id_type=MESH)

    feature_load.wait()
    gain_load.wait()
    floated = features[...].astype(jnp.float32)
    squares = jnp.sum(floated * floated, axis=1, keepdims=True)
    square_rows = jnp.transpose(jnp.broadcast_to(squares, (tokens, tokens)))[:8]
    square_send[...] = square_rows

    pl.semaphore_wait(barrier, sections + jnp.where(pair > 0, 1, 0) + jnp.where(pair < pairs - 1, 1, 0))

    def square_copy(k):
        return pltpu.make_async_remote_copy(
            src_ref=square_send, dst_ref=square_recv.at[k - 1],
            send_sem=sq_send.at[k - 1], recv_sem=sq_recv.at[k - 1],
            device_id={"section": flipped(section, k, sections)}, device_id_type=MESH,
        )

    def part_copy(g, k):
        return pltpu.make_async_remote_copy(
            src_ref=send_buf.at[g, k - 1], dst_ref=recv_buf.at[g, k - 1],
            send_sem=rs_send.at[g, k - 1], recv_sem=rs_recv.at[g, k - 1],
            device_id={"section": flipped(section, k, sections)}, device_id_type=MESH,
        )

    def chain_copy(g, hop):
        place = kv_ref.at[g, shard - CORES * hop]
        return pltpu.make_async_remote_copy(
            src_ref=place, dst_ref=place,
            send_sem=chain_send.at[g, hop], recv_sem=chain_recv.at[g, hop],
            device_id={"seq": later}, device_id_type=MESH,
        )

    def twin_copy(g, hop):
        place = kv_ref.at[g, shard - CORES * hop]
        return pltpu.make_async_remote_copy(
            src_ref=place, dst_ref=place,
            send_sem=twin_send.at[g, hop], recv_sem=twin_recv.at[g, hop],
            device_id={"seq": twin}, device_id_type=MESH,
        )

    def chain_arrival(g, hop):
        place = kv_ref.at[g, shard - CORES * hop]
        return pltpu.make_async_remote_copy(
            src_ref=place, dst_ref=place,
            send_sem=chain_send.at[g, hop - 1], recv_sem=chain_recv.at[g, hop - 1],
            device_id={"seq": later}, device_id_type=MESH,
        )

    def twin_arrival(g, hop):
        place = kv_ref.at[g, twin - CORES * hop]
        return pltpu.make_async_remote_copy(
            src_ref=place, dst_ref=place,
            send_sem=twin_send.at[g, hop], recv_sem=twin_recv.at[g, hop],
            device_id={"seq": twin}, device_id_type=MESH,
        )

    for k in range(1, sections):
        square_copy(k).start()
    total = square_rows
    for k in range(1, sections):
        square_copy(k).wait()
        total = total + square_recv[k - 1]
    mean = jnp.transpose(jnp.broadcast_to(total[:1], (tokens, tokens))) / feature_width
    inverse = lax.rsqrt(mean + 1e-05)
    for first in range(0, features.shape[1], tokens):
        part = pl.ds(first, tokens)
        scaled[:, part] = (
            features[:, part].astype(jnp.float32) * inverse * gain[:, part]
        ).astype(jnp.bfloat16)

    for slot, (g, k) in enumerate(order):
        weight_copy(slot).wait()
        part = jnp.dot(scaled[...], weight_buf[slot], preferred_element_type=jnp.float32)
        if k:
            send_buf[g, k - 1] = part.astype(jnp.bfloat16)
            part_copy(g, k).start()
        else:
            own_part[g] = part

    for g in range(groups):
        summed = own_part[g]
        for k in range(sections - 1, 0, -1):
            part_copy(g, k).wait_recv()
            summed = summed + recv_buf[g, k - 1].astype(jnp.float32)
        kv_ref[g, shard] = summed.astype(jnp.bfloat16)

        @pl.when(pair < pairs - 1)
        def _():
            chain_copy(g, 0).start()

        twin_copy(g, 0).start()

    for hop in range(1, pairs):
        @pl.when(hop <= pair)
        def _():
            for g in range(groups):
                chain_arrival(g, hop).wait_recv()

                @pl.when(pair < pairs - 1)
                def _():
                    chain_copy(g, hop).start()

                twin_copy(g, hop).start()

    for hop in range(pairs):
        @pl.when(hop <= pair)
        def _():
            for g in range(groups):
                twin_arrival(g, hop).wait_recv()
                twin_copy(g, hop).wait_send()

                @pl.when(pair < pairs - 1)
                def _():
                    chain_copy(g, hop).wait_send()

    for g in range(groups):
        for k in range(1, sections):
            part_copy(g, k).wait_send()


def attend_kernel(
    block_len,
    doc_smem, list_smem, docs_ref, query_ref, step_ref, kv_ref, out_ref, cache_ref,
    bias, step_scores, scores, top, acc,
):
    shard = lax.axis_index("seq")
    step, group = pl.program_id(0), pl.program_id(1)
    _, heads, tokens, head_dim = query_ref.shape
    steps = step_ref.shape[0]
    groups, shards = kv_ref.shape[:2]
    entries = list_smem.shape[2]
    chunk = CORES * tokens
    chunks = shards // CORES
    pair = shard // CORES
    scale = math.log2(math.e) / math.sqrt(head_dim)
    contract_last = (((1,), (1,)), ((), ()))
    rows = [slice(h * tokens, (h + 1) * tokens) for h in range(heads)]

    first_doc = doc_smem[shard * tokens]
    lowest = jnp.int32(0)
    for c in range(chunks):
        lowest = lowest + jnp.where(doc_smem[c * chunk + chunk - 1] < first_doc, 1, 0)

    row = lax.broadcasted_iota(jnp.int32, (tokens, tokens), 0)
    column = lax.broadcasted_iota(jnp.int32, (tokens, tokens), 1)
    row_blocks = tokens // block_len

    @pl.when(group == 0)
    def _():
        for g in range(groups):
            cache_ref[g] = kv_ref[g, shard]
        lane = lax.broadcasted_iota(jnp.int32, (1, tokens), 1)
        own_docs = docs_ref[pl.ds(shard, 1), :].astype(jnp.float32)
        row_docs = jnp.transpose(jnp.broadcast_to(own_docs, (tokens, tokens)))

        def fill(c, _):
            for half in range(CORES):
                key_shard = c * CORES + half
                key_block = key_shard * row_blocks + lane // block_len
                listed = []
                for r in range(row_blocks):
                    marks = jnp.full((1, tokens), neg_fill, jnp.float32)
                    for e in range(entries):
                        entry = list_smem[step, shard * row_blocks + r, e]
                        marks = jnp.where(key_block == entry, 0.0, marks)
                    listed.append(marks)
                marks = jnp.broadcast_to(listed[-1], (tokens, tokens))
                for r in range(row_blocks - 2, -1, -1):
                    marks = jnp.where(row < (r + 1) * block_len, listed[r], marks)
                key_docs = docs_ref[pl.ds(key_shard, 1), :].astype(jnp.float32)
                marks = jnp.where(row_docs == key_docs, marks, neg_fill)
                marks = jnp.where(key_shard * tokens + column <= shard * tokens + row, marks, neg_fill)
                bias[c, :, half * tokens:(half + 1) * tokens] = marks
            return 0

        lax.fori_loop(lowest, pair + 1, fill, 0)

    queries = query_ref[0].reshape(heads * tokens, head_dim)
    diagonal = jnp.where(row == column, 0.0, neg_fill)

    def score(keys):
        return lax.dot_general(queries, keys, contract_last, preferred_element_type=jnp.float32)

    def extended(values):
        return jnp.concatenate([values, jnp.ones_like(values)], axis=1)

    def step_first(m):
        found = score(step_ref[m, group, :, :head_dim])
        for r in rows:
            masked = found[r] + diagonal
            step_scores[m, r, :] = masked
            top[r, :] = jnp.maximum(top[r, :], masked) if m else masked

    def step_second(m):
        weights = [
            jnp.exp2(step_scores[m, r, :] * scale - top[r, :]).astype(jnp.bfloat16) for r in rows
        ]
        return jnp.dot(
            jnp.concatenate(weights, axis=0), extended(step_ref[m, group, :, head_dim:]),
            preferred_element_type=jnp.float32,
        )

    def first_pass(c, many):
        keys = kv_ref[group, pl.ds(c * CORES, many * CORES), :, :head_dim].reshape(many * chunk, head_dim)
        found = score(keys)
        for r in rows:
            highest = top[r, :]
            for i in range(many):
                masked = found[r, i * chunk:(i + 1) * chunk] + bias[c + i]
                scores[c + i, r, :] = masked
                highest = jnp.maximum(highest, jnp.maximum(masked[:, :tokens], masked[:, tokens:]))
            top[r, :] = highest

    def second_pass(c, many):
        values = kv_ref[group, pl.ds(c * CORES, many * CORES), :, head_dim:].reshape(many * chunk, head_dim)
        weights = []
        for r in rows:
            highest = jnp.concatenate([top[r, :]] * CORES, axis=1)
            weights.append(jnp.concatenate(
                [jnp.exp2(scores[c + i, r, :] * scale - highest).astype(jnp.bfloat16) for i in range(many)],
                axis=1,
            ))
        acc[...] += jnp.dot(
            jnp.concatenate(weights, axis=0), extended(values), preferred_element_type=jnp.float32
        )

    def over_chunks(run):
        count = pair + 1 - lowest

        def body(i, _):
            run(lowest + 2 * i, 2)
            return 0

        lax.fori_loop(0, count // 2, body, 0)

        @pl.when(count % 2 == 1)
        def _():
            run(pair, 1)

    step_first(0)
    for m in range(1, steps):
        pl.when(m <= step)(functools.partial(step_first, m))
    over_chunks(first_pass)

    for r in rows:
        highest = jnp.max(top[r, :], axis=1, keepdims=True) * scale
        top[r, :] = jnp.broadcast_to(highest, (tokens, tokens))

    acc[...] = step_second(0)
    for m in range(1, steps):
        @pl.when(m <= step)
        def _():
            acc[...] += step_second(m)
    over_chunks(second_pass)

    for h, r in enumerate(rows):
        out_ref[0, h] = (acc[r, :head_dim] / acc[r, head_dim:]).astype(out_ref.dtype)


def per_device(sections, shards, features, norm_gain, kv_weight, queries, step_kv, doc_ids, block_lists):
    steps, local_heads, tokens, head_dim = queries.shape
    groups = step_kv.shape[1]
    group_size = local_heads // groups
    width = 2 * head_dim
    local_width = features.shape[1]
    blocks = block_lists.shape[1]
    block_len = doc_ids.shape[0] // blocks
    pairs = shards // CORES
    others = sections - 1
    dma = pltpu.SemaphoreType.DMA
    vmem = pl.BlockSpec(memory_space=pltpu.VMEM)

    kv_all = pl.pallas_call(
        functools.partial(kv_kernel, sections, shards, local_width * sections),
        out_shape=jax.ShapeDtypeStruct((groups, shards, tokens, width), jnp.bfloat16),
        in_specs=[pl.BlockSpec(memory_space=pl.ANY)] * 3,
        out_specs=vmem,
        scratch_shapes=[
            pltpu.VMEM((tokens, local_width), jnp.bfloat16),
            pltpu.VMEM((1, local_width), jnp.float32),
            pltpu.VMEM((groups * sections, local_width, width), jnp.bfloat16),
            pltpu.VMEM((tokens, local_width), jnp.bfloat16),
            pltpu.VMEM((groups, tokens, width), jnp.float32),
            pltpu.VMEM((groups, others, tokens, width), jnp.bfloat16),
            pltpu.VMEM((groups, others, tokens, width), jnp.bfloat16),
            pltpu.VMEM((8, tokens), jnp.float32),
            pltpu.VMEM((others, 8, tokens), jnp.float32),
            dma((2,)),
            dma((groups * sections,)),
            dma((groups, others)),
            dma((groups, others)),
            dma((others,)),
            dma((others,)),
            dma((groups, pairs)),
            dma((groups, pairs)),
            dma((groups, pairs)),
            dma((groups, pairs)),
        ],
        compiler_params=pltpu.CompilerParams(
            collective_id=0, has_side_effects=True, vmem_limit_bytes=60 * 1024 * 1024
        ),
    )(features, norm_gain.reshape(1, local_width), kv_weight)

    smem = pl.BlockSpec(memory_space=pltpu.SMEM)
    attended, kv_cache = pl.pallas_call(
        functools.partial(attend_kernel, block_len),
        grid=(steps, groups),
        out_shape=(
            jax.ShapeDtypeStruct(queries.shape, jnp.bfloat16),
            jax.ShapeDtypeStruct((groups, tokens, width), jnp.bfloat16),
        ),
        in_specs=[
            smem,
            smem,
            vmem,
            pl.BlockSpec((1, group_size, tokens, head_dim), lambda s, g: (s, g, 0, 0)),
            vmem,
            vmem,
        ],
        out_specs=(
            pl.BlockSpec((1, group_size, tokens, head_dim), lambda s, g: (s, g, 0, 0)),
            vmem,
        ),
        scratch_shapes=[
            pltpu.VMEM((pairs, tokens, CORES * tokens), jnp.float32),
            pltpu.VMEM((steps, group_size * tokens, tokens), jnp.float32),
            pltpu.VMEM((pairs, group_size * tokens, CORES * tokens), jnp.float32),
            pltpu.VMEM((group_size * tokens, tokens), jnp.float32),
            pltpu.VMEM((group_size * tokens, width), jnp.float32),
        ],
        compiler_params=pltpu.CompilerParams(vmem_limit_bytes=48 * 1024 * 1024),
    )(
        doc_ids,
        block_lists,
        doc_ids.reshape(shards, tokens),
        queries,
        step_kv,
        kv_all,
    )
    return (attended, kv_cache)


def solution(mesh):
    in_specs = (
        P("seq", "section"),
        P("section"),
        P("section", None),
        P(None, "section", "seq", None),
        P(None, "section", "seq", None),
        P(),
        P(),
    )
    out_specs = (P(None, "section", "seq", None), P("section", "seq", None))
    body = functools.partial(per_device, mesh.shape["section"], mesh.shape["seq"])
    return jax.shard_map(body, mesh=mesh, in_specs=in_specs, out_specs=out_specs, check_vma=False)
```

time: 53.2 us -> 48.7 us (0.915)
  local copies, waits for them, and re-layouts: 5.94 us -> 1.23 us
    pallas_call x1, Pallas kernels: 20.9 us -> 25.3 us  [per_device(): pl.pallas_call(functools.partial(kv_kernel, sections, shards, local_width...]
    pallas_call x1, Pallas kernels: 24.9 us -> 20.9 us  [per_device(): pl.pallas_call(functools.partial(attend_kernel, block_len), grid=(steps,...]
    unnamed x12 -> x10, local copies, waits for them, and re-layouts: 5.13 us -> 1.23 us
    reshape x1 -> x0, local copies, waits for them, and re-layouts: 0.81 us -> none  [per_device(): block_lists.reshape(-1)]
where the time goes in v2:
time: 48.7 us; the launch traced here: 48.2 us
  Pallas kernels  46.2 us (95%)
  local copies, waits for them, and re-layouts  1.23 us (3%)
  between operations  0.71 us (1%)
    pallas_call x1, Pallas kernels, per_device(): pl.pallas_call(functools.partial(kv_kernel, sections, shards, local_width...  25.3 us
    pallas_call x1, Pallas kernels, per_device(): pl.pallas_call(functools.partial(attend_kernel, block_len), grid=(steps,...  20.9 us
    unnamed x10, local copies, waits for them, and re-layouts  1.23 us

profile of v2, /device:TPU:24, one launch (start us, length us, event | category | flops | bytes accessed | tf_op | source)
XLA Modules:
  0.0 48.2 jit_solution(7051199220908978796)
XLA Ops:
  0.6 0.0 copy-start.1
  0.6 0.0 copy-start.2
  0.7 0.0 copy-start.3
  0.7 0.0 copy-start.4
  0.7 25.3 %shard_map.86.kv_ref = bf16[2,8,128,256]{3,2,1,0:T(8,128)(2,1)} custom-call(bf16[128,2048]{1,0:T(8,128)(2,1)} %feat_ref.1, f32[1,2048]{1,0:T(1,128)} %bitcast.3, bf16[2048,2048]{1,0:T(8,128)(2,1)} %weight_ref.1), custom_call_target="tpu_custom_call" | custom-call | tf_op jit(solution)/shard_map/pallas_call | solution.py:340
  26.0 0.0 copy-done.1
  26.0 0.0 copy-done.2
  26.0 0.0 copy-done.3
  26.0 0.0 copy-done.4
  26.0 0.0 copy-start
  26.0 1.2 %copy-done = bf16[2,8,128,256]{3,2,1,0:T(8,128)(2,1)S(1)} copy-done((bf16[2,8,128,256]{3,2,1,0:T(8,128)(2,1)S(1)}, bf16[2,8,128,256]{3,2,1,0:T(8,128)(2,1)}, u32[]{:S(2)}) %copy-start) | copy-done | bytes 1048600
  27.3 20.9 %shard_map.87 = (bf16[3,16,128,128]{3,2,1,0:T(8,128)(2,1)}, bf16[2,128,256]{2,1,0:T(8,128)(2,1)}) custom-call(s32[1024]{0:T(1024)S(1)} %copy-done.4, s32[3,16,16]{2,1,0:T(8,128)S(1)} %copy-done.3, s32[8,128]{1,0:T(8,128)S(1)} %bitcast.2, bf16[3,16,128,128]{3,2,1,0:T(8,128)(2,1)S(1)} %copy-done.1, bf16[3,2,128,256]{3,2,1,0:T(8,128)(2,1)S(1)} %copy-done.2, ...), custom_call_target="tpu_custom_call" | custom-call | tf_op jit(solution)/shard_map/pallas_call | solution.py:372
Async XLA Ops:
  0.6 25.4 %copy-start.1 = (bf16[3,16,128,128]{3,2,1,0:T(8,128)(2,1)S(1)}, bf16[3,16,128,128]{3,2,1,0:T(8,128)(2,1)}, u32[]{:S(2)}) copy-start(bf16[3,16,128,128]{3,2,1,0:T(8,128)(2,1)} %query_ref.1) | copy-start | bytes 4718596
  0.6 25.4 %copy-start.2 = (bf16[3,2,128,256]{3,2,1,0:T(8,128)(2,1)S(1)}, bf16[3,2,128,256]{3,2,1,0:T(8,128)(2,1)}, u32[]{:S(2)}) copy-start(bf16[3,2,128,256]{3,2,1,0:T(8,128)(2,1)} %step_ref.1) | copy-start | bytes 1179652
  0.7 25.4 %copy-start.3 = (s32[3,16,16]{2,1,0:T(8,128)S(1)}, s32[3,16,16]{2,1,0:T(8,128)}, u32[]{:S(2)}) copy-start(s32[3,16,16]{2,1,0:T(8,128)} %list_smem.1) | copy-start | bytes 9220
  0.7 25.4 %copy-start.4 = (s32[1024]{0:T(1024)S(1)}, s32[1024]{0:T(1024)}, u32[]{:S(2)}) copy-start(s32[1024]{0:T(1024)} %doc_smem.1) | copy-start | bytes 12292
  26.0 1.2 %copy-start = (bf16[2,8,128,256]{3,2,1,0:T(8,128)(2,1)S(1)}, bf16[2,8,128,256]{3,2,1,0:T(8,128)(2,1)}, u32[]{:S(2)}) copy-start(bf16[2,8,128,256]{3,2,1,0:T(8,128)(2,1)} %shard_map.86.kv_ref) | copy-start | bytes 3145732

commit v3 on v2

v3 whole, which is shorter than its diff:
```python
import functools
import math

import jax
import jax.numpy as jnp
from jax import lax
from jax.experimental import pallas as pl
from jax.experimental.pallas import tpu as pltpu
from jax.sharding import PartitionSpec as P

neg_fill = -1e30
MESH = pl.DeviceIdType.MESH
CORES = 2


def flipped(index, mask, count):
    result, bit = 0, 1
    while bit < count:
        own = (index // bit) % 2
        result = result + bit * ((1 - own) if mask & bit else own)
        bit *= 2
    return result


def fused_kernel(
    sections, shards, feature_width, block_len,
    feat_ref, gain_ref, weight_ref, query_ref, step_ref, docs_ref, list_smem,
    out_ref, cache_ref,
    features, gain, queries, step_kv, weight_buf, scaled, own_part, send_buf, recv_buf,
    square_send, square_recv, kv, bias, top, acc,
    load_sem, weight_sem, rs_send, rs_recv, sq_send, sq_recv,
    direct_send, direct_recv, twin_send, twin_recv,
):
    section = lax.axis_index("section")
    shard = lax.axis_index("seq")
    groups, _, tokens, width = kv.shape
    steps, local_heads, _, head_dim = queries.shape
    heads = local_heads // groups
    entries = list_smem.shape[2]
    chunk = CORES * tokens
    pairs = shards // CORES
    pair, core = shard // CORES, shard % CORES
    twin = pair * CORES + 1 - core
    scale = math.log2(math.e) / math.sqrt(head_dim)
    order = [(g, k) for g in range(groups) for k in range(sections - 1, -1, -1)]
    row_blocks = tokens // block_len

    def weight_copy(slot):
        g, k = order[slot]
        column = pl.multiple_of((flipped(section, k, sections) * groups + g) * width, width)
        return pltpu.make_async_copy(
            weight_ref.at[:, pl.ds(column, width)], weight_buf.at[slot], weight_sem.at[slot]
        )

    feature_load = pltpu.make_async_copy(feat_ref, features, load_sem.at[0])
    gain_load = pltpu.make_async_copy(gain_ref, gain, load_sem.at[1])
    step_load = pltpu.make_async_copy(step_ref, step_kv, load_sem.at[2])
    query_load = pltpu.make_async_copy(query_ref, queries, load_sem.at[3])
    for load in (feature_load, gain_load, step_load, query_load):
        load.start()
    for slot in range(len(order)):
        weight_copy(slot).start()

    barrier = pltpu.get_barrier_semaphore()
    for k in range(1, sections):
        pl.semaphore_signal(
            barrier, inc=1, device_id={"section": flipped(section, k, sections)}, device_id_type=MESH
        )
    pl.semaphore_signal(barrier, inc=1, device_id={"seq": twin}, device_id_type=MESH)
    for d in range(1, pairs):
        other = (pair + d) % pairs * CORES + core
        pl.semaphore_signal(barrier, inc=1, device_id={"seq": other}, device_id_type=MESH)

    feature_load.wait()
    gain_load.wait()
    floated = features[...].astype(jnp.float32)
    squares = jnp.sum(floated * floated, axis=1, keepdims=True)
    square_rows = jnp.transpose(jnp.broadcast_to(squares, (tokens, tokens)))[:8]
    square_send[...] = square_rows

    pl.semaphore_wait(barrier, sections + pairs - 1)

    def square_copy(k):
        return pltpu.make_async_remote_copy(
            src_ref=square_send, dst_ref=square_recv.at[k - 1],
            send_sem=sq_send.at[k - 1], recv_sem=sq_recv.at[k - 1],
            device_id={"section": flipped(section, k, sections)}, device_id_type=MESH,
        )

    def part_copy(g, k):
        return pltpu.make_async_remote_copy(
            src_ref=send_buf.at[g, k - 1], dst_ref=recv_buf.at[g, k - 1],
            send_sem=rs_send.at[g, k - 1], recv_sem=rs_recv.at[g, k - 1],
            device_id={"section": flipped(section, k, sections)}, device_id_type=MESH,
        )

    def direct_copy(g, d):
        place = kv.at[g, shard]
        return pltpu.make_async_remote_copy(
            src_ref=place, dst_ref=place,
            send_sem=direct_send.at[g, d], recv_sem=direct_recv.at[g, d],
            device_id={"seq": shard + CORES * d}, device_id_type=MESH,
        )

    def direct_arrival(g, d):
        place = kv.at[g, shard - CORES * d]
        return pltpu.make_async_remote_copy(
            src_ref=place, dst_ref=place,
            send_sem=direct_send.at[g, d], recv_sem=direct_recv.at[g, d],
            device_id={"seq": twin}, device_id_type=MESH,
        )

    def twin_copy(g, hop):
        place = kv.at[g, shard - CORES * hop]
        return pltpu.make_async_remote_copy(
            src_ref=place, dst_ref=place,
            send_sem=twin_send.at[g, hop], recv_sem=twin_recv.at[g, hop],
            device_id={"seq": twin}, device_id_type=MESH,
        )

    def twin_arrival(g, hop):
        place = kv.at[g, twin - CORES * hop]
        return pltpu.make_async_remote_copy(
            src_ref=place, dst_ref=place,
            send_sem=twin_send.at[g, hop], recv_sem=twin_recv.at[g, hop],
            device_id={"seq": twin}, device_id_type=MESH,
        )

    def own_steps(h, _):
        g = h // heads
        part = pl.ds(pl.multiple_of(h % heads * tokens, tokens), tokens)
        keys = [step_kv[m, g, :, :head_dim].astype(jnp.float32) for m in range(steps)]
        values = [step_kv[m, g, :, head_dim:].astype(jnp.float32) for m in range(steps)]
        for s in range(steps):
            query = queries[s, h].astype(jnp.float32)
            found = [jnp.sum(query * keys[m], axis=1, keepdims=True) * scale for m in range(s + 1)]
            highest = functools.reduce(jnp.maximum, found)
            weights = [jnp.exp2(one - highest) for one in found]
            rounded = [w.astype(jnp.bfloat16).astype(jnp.float32) for w in weights]
            top[s, g, part, :] = jnp.broadcast_to(highest, (tokens, tokens))
            acc[s, g, part, :head_dim] = sum(w * values[m] for m, w in enumerate(rounded))
            acc[s, g, part, head_dim:] = jnp.broadcast_to(sum(weights), (tokens, head_dim))
        return 0

    def fill_bias(c, _):
        row = lax.broadcasted_iota(jnp.int32, (tokens, tokens), 0)
        column = lax.broadcasted_iota(jnp.int32, (tokens, tokens), 1)
        lane = lax.broadcasted_iota(jnp.int32, (1, tokens), 1)
        own_docs = docs_ref[pl.ds(shard, 1), :].astype(jnp.float32)
        row_docs = jnp.transpose(jnp.broadcast_to(own_docs, (tokens, tokens)))
        for half in range(CORES):
            key_shard = c * CORES + half
            key_block = key_shard * row_blocks + lane // block_len
            key_docs = docs_ref[pl.ds(key_shard, 1), :].astype(jnp.float32)
            shared = (row_docs == key_docs) & (key_shard * tokens + column <= shard * tokens + row)
            for s in range(steps):
                listed = []
                for r in range(row_blocks):
                    marks = jnp.full((1, tokens), neg_fill, jnp.float32)
                    for e in range(entries):
                        entry = list_smem[s, shard * row_blocks + r, e]
                        marks = jnp.where(key_block == entry, 0.0, marks)
                    listed.append(marks)
                marks = jnp.broadcast_to(listed[-1], (tokens, tokens))
                for r in range(row_blocks - 2, -1, -1):
                    marks = jnp.where(row < (r + 1) * block_len, listed[r], marks)
                bias[s, c, :, half * tokens:(half + 1) * tokens] = jnp.where(shared, marks, neg_fill)
        return 0

    for k in range(1, sections):
        square_copy(k).start()

    step_load.wait()
    query_load.wait()
    lax.fori_loop(0, local_heads // 2, own_steps, 0)

    total = square_rows
    for k in range(1, sections):
        square_copy(k).wait()
        total = total + square_recv[k - 1]
    mean = jnp.transpose(jnp.broadcast_to(total[:1], (tokens, tokens))) / feature_width
    inverse = lax.rsqrt(mean + 1e-05)
    for first in range(0, features.shape[1], tokens):
        part = pl.ds(first, tokens)
        scaled[:, part] = (
            features[:, part].astype(jnp.float32) * inverse * gain[:, part]
        ).astype(jnp.bfloat16)

    for slot, (g, k) in enumerate(order):
        weight_copy(slot).wait()
        part = jnp.dot(scaled[...], weight_buf[slot], preferred_element_type=jnp.float32)
        if k:
            send_buf[g, k - 1] = part.astype(jnp.bfloat16)
            part_copy(g, k).start()
        else:
            own_part[g] = part

    lax.fori_loop(local_heads // 2, local_heads, own_steps, 0)
    lax.fori_loop(0, pair + 1, fill_bias, 0)

    for g in range(groups):
        summed = own_part[g]
        for k in range(sections - 1, 0, -1):
            part_copy(g, k).wait_recv()
            summed = summed + recv_buf[g, k - 1].astype(jnp.float32)
        rounded = summed.astype(jnp.bfloat16)
        kv[g, shard] = rounded
        cache_ref[g] = rounded
        twin_copy(g, 0).start()

        def send(d, _):
            direct_copy(g, d).start()
            return 0

        lax.fori_loop(1, pairs - pair, send, 0)

    def attend(s, g, c):
        keys = kv[g, pl.ds(c * CORES, CORES), :, :head_dim].reshape(chunk, head_dim)
        values = kv[g, pl.ds(c * CORES, CORES), :, head_dim:].reshape(chunk, head_dim)
        extended = jnp.concatenate([values, jnp.ones_like(values)], axis=1)
        asked = queries[s, pl.ds(g * heads, heads)].reshape(heads * tokens, head_dim)
        found = lax.dot_general(
            asked, keys, (((1,), (1,)), ((), ())), preferred_element_type=jnp.float32
        )
        weights, factors = [], []
        rows = [slice(h * tokens, (h + 1) * tokens) for h in range(heads)]
        for r in rows:
            masked = found[r] * scale + bias[s, c]
            largest = jnp.max(jnp.maximum(masked[:, :tokens], masked[:, tokens:]), axis=1, keepdims=True)
            before = top[s, g, r, :]
            highest = jnp.maximum(before, largest)
            top[s, g, r, :] = highest
            factors.append(jnp.exp2(before - highest))
            weights.append(
                jnp.exp2(masked - jnp.concatenate([highest] * CORES, axis=1)).astype(jnp.bfloat16)
            )
        added = jnp.dot(jnp.concatenate(weights, axis=0), extended, preferred_element_type=jnp.float32)
        for r, factor in zip(rows, factors):
            acc[s, g, r, :] = acc[s, g, r, :] * jnp.concatenate([factor] * CORES, axis=1) + added[r]

    def over_steps(g, c):
        def body(s, _):
            attend(s, g, c)
            return 0

        lax.fori_loop(0, steps, body, 0)

    for g in range(groups):
        twin_arrival(g, 0).wait_recv()

    def hop_body(hop, _):
        c = pair - hop
        for g in range(groups):
            over_steps(g, c)
            if g == 0:
                @pl.when(hop < pair)
                def _():
                    for each in range(groups):
                        direct_arrival(each, hop + 1).wait_recv()
                        twin_copy(each, hop + 1).start()

        @pl.when(hop < pair)
        def _():
            for each in range(groups):
                twin_arrival(each, hop + 1).wait_recv()

        return 0

    lax.fori_loop(0, pair + 1, hop_body, 0)

    def finish(i, _):
        s, h = i // local_heads, i % local_heads
        g = h // heads
        part = pl.ds(pl.multiple_of(h % heads * tokens, tokens), tokens)
        out_ref[s, h] = (acc[s, g, part, :head_dim] / acc[s, g, part, head_dim:]).astype(out_ref.dtype)
        return 0

    lax.fori_loop(0, steps * local_heads, finish, 0)

    for g in range(groups):
        for k in range(1, sections):
            part_copy(g, k).wait_send()

        def sent(d, _):
            direct_copy(g, d).wait_send()
            return 0

        def passed(hop, _):
            twin_copy(g, hop).wait_send()
            return 0

        lax.fori_loop(1, pairs - pair, sent, 0)
        lax.fori_loop(0, pair + 1, passed, 0)


def per_device(sections, shards, features, norm_gain, kv_weight, queries, step_kv, doc_ids, block_lists):
    steps, local_heads, tokens, head_dim = queries.shape
    groups = step_kv.shape[1]
    rows = local_heads // groups * tokens
    width = 2 * head_dim
    local_width = features.shape[1]
    blocks = block_lists.shape[1]
    block_len = doc_ids.shape[0] // blocks
    pairs = shards // CORES
    others = sections - 1
    dma = pltpu.SemaphoreType.DMA
    vmem = pl.BlockSpec(memory_space=pltpu.VMEM)
    anywhere = pl.BlockSpec(memory_space=pl.ANY)
    return pl.pallas_call(
        functools.partial(fused_kernel, sections, shards, local_width * sections, block_len),
        out_shape=(
            jax.ShapeDtypeStruct(queries.shape, jnp.bfloat16),
            jax.ShapeDtypeStruct((groups, tokens, width), jnp.bfloat16),
        ),
        in_specs=[anywhere] * 5 + [vmem, pl.BlockSpec(memory_space=pltpu.SMEM)],
        out_specs=(vmem, vmem),
        scratch_shapes=[
            pltpu.VMEM((tokens, local_width), jnp.bfloat16),
            pltpu.VMEM((1, local_width), jnp.float32),
            pltpu.VMEM(queries.shape, jnp.bfloat16),
            pltpu.VMEM(step_kv.shape, jnp.bfloat16),
            pltpu.VMEM((groups * sections, local_width, width), jnp.bfloat16),
            pltpu.VMEM((tokens, local_width), jnp.bfloat16),
            pltpu.VMEM((groups, tokens, width), jnp.float32),
            pltpu.VMEM((groups, others, tokens, width), jnp.bfloat16),
            pltpu.VMEM((groups, others, tokens, width), jnp.bfloat16),
            pltpu.VMEM((8, tokens), jnp.float32),
            pltpu.VMEM((others, 8, tokens), jnp.float32),
            pltpu.VMEM((groups, shards, tokens, width), jnp.bfloat16),
            pltpu.VMEM((steps, pairs, tokens, CORES * tokens), jnp.float32),
            pltpu.VMEM((steps, groups, rows, tokens), jnp.float32),
            pltpu.VMEM((steps, groups, rows, width), jnp.float32),
            dma((4,)),
            dma((groups * sections,)),
            dma((groups, others)),
            dma((groups, others)),
            dma((others,)),
            dma((others,)),
            dma((groups, pairs)),
            dma((groups, pairs)),
            dma((groups, pairs)),
            dma((groups, pairs)),
        ],
        compiler_params=pltpu.CompilerParams(
            collective_id=0, has_side_effects=True, vmem_limit_bytes=60 * 1024 * 1024
        ),
    )(
        features,
        norm_gain.reshape(1, local_width),
        kv_weight,
        queries,
        step_kv,
        doc_ids.reshape(shards, tokens),
        block_lists,
    )


def solution(mesh):
    in_specs = (
        P("seq", "section"),
        P("section"),
        P("section", None),
        P(None, "section", "seq", None),
        P(None, "section", "seq", None),
        P(),
        P(),
    )
    out_specs = (P(None, "section", "seq", None), P("section", "seq", None))
    body = functools.partial(per_device, mesh.shape["section"], mesh.shape["seq"])
    return jax.shard_map(body, mesh=mesh, in_specs=in_specs, out_specs=out_specs, check_vma=False)
```

time: 48.7 us -> 42.9 us (0.88)
  Pallas kernels: 46.2 us -> 38.5 us
  local copies, waits for them, and re-layouts: 1.23 us -> 3.42 us
    pallas_call x2 -> x1, Pallas kernels: 46.2 us -> 38.5 us  [per_device(): pl.pallas_call(functools.partial(fused_kernel, sections, shards, local_wi...]
    unnamed x10 -> x4, local copies, waits for them, and re-layouts: 1.23 us -> 3.42 us
where the time goes in v3:
time: 42.9 us; the launch traced here: 42.6 us
  Pallas kernels  38.5 us (90%)
  local copies, waits for them, and re-layouts  3.42 us (8%)
  between operations  0.65 us (2%)
    pallas_call x1, Pallas kernels, per_device(): pl.pallas_call(functools.partial(fused_kernel, sections, shards, local_wi...  38.5 us
    unnamed x4, local copies, waits for them, and re-layouts  3.42 us

profile of v3, /device:TPU:24, one launch (start us, length us, event | category | flops | bytes accessed | tf_op | source)
XLA Modules:
  0.0 42.6 jit_solution(14972832477225746662)
XLA Ops:
  0.6 38.5 %shard_map.86 = (bf16[3,16,128,128]{3,2,1,0:T(8,128)(2,1)}, bf16[2,128,256]{2,1,0:T(8,128)(2,1)}) custom-call(bf16[128,2048]{1,0:T(8,128)(2,1)} %feat_ref.1, f32[1,2048]{1,0:T(1,128)} %bitcast.2, bf16[2048,2048]{1,0:T(8,128)(2,1)} %weight_ref.1, bf16[3,16,128,128]{3,2,1,0:T(8,128)(2,1)} %query_ref.1, bf16[3,2,128,256]{3,2,1,0:T(8,128)(2,1)} %step_ref.1, ...), custom_call_target="tpu_custom_call" | custom-call | tf_op jit(solution)/shard_map/pallas_call | solution.py:309
  39.2 0.0 copy-start
  39.2 2.8 %copy.11 = bf16[3,16,128,128]{3,2,1,0:T(8,128)(2,1)} copy(bf16[3,16,128,128]{3,2,1,0:T(8,128)(2,1)} %get-tuple-element.4) | data formatting | bytes 3145728
  42.0 0.0 copy-done
  42.0 0.7 %copy.12 = bf16[2,128,256]{2,1,0:T(8,128)(2,1)} copy(bf16[2,128,256]{2,1,0:T(8,128)(2,1)S(1)} %copy-done) | data formatting | bytes 262144
Async XLA Ops:
  39.2 2.8 %copy-start = (bf16[2,128,256]{2,1,0:T(8,128)(2,1)S(1)}, bf16[2,128,256]{2,1,0:T(8,128)(2,1)}, u32[]{:S(2)}) copy-start(bf16[2,128,256]{2,1,0:T(8,128)(2,1)} %get-tuple-element.5) | copy-start | bytes 393220

commit v4 on v3

--- a/solution.py
+++ b/solution.py
@@ -42,14 +42,14 @@
     pair, core = shard // CORES, shard % CORES
     twin = pair * CORES + 1 - core
     scale = math.log2(math.e) / math.sqrt(head_dim)
-    order = [(g, k) for g in range(groups) for k in range(sections - 1, -1, -1)]
+    order = list(range(sections - 1, -1, -1))
+    span = groups * width
     row_blocks = tokens // block_len
 
     def weight_copy(slot):
-        g, k = order[slot]
-        column = pl.multiple_of((flipped(section, k, sections) * groups + g) * width, width)
+        column = pl.multiple_of(flipped(section, order[slot], sections) * span, span)
         return pltpu.make_async_copy(
-            weight_ref.at[:, pl.ds(column, width)], weight_buf.at[slot], weight_sem.at[slot]
+            weight_ref.at[:, pl.ds(column, span)], weight_buf.at[slot], weight_sem.at[slot]
         )
 
     feature_load = pltpu.make_async_copy(feat_ref, features, load_sem.at[0])
@@ -172,7 +172,7 @@
 
     step_load.wait()
     query_load.wait()
-    lax.fori_loop(0, local_heads // 2, own_steps, 0)
+    lax.fori_loop(0, local_heads // 4, own_steps, 0)
 
     total = square_rows
     for k in range(1, sections):
@@ -186,17 +186,19 @@
             features[:, part].astype(jnp.float32) * inverse * gain[:, part]
         ).astype(jnp.bfloat16)
 
-    for slot, (g, k) in enumerate(order):
+    for slot, k in enumerate(order):
         weight_copy(slot).wait()
         part = jnp.dot(scaled[...], weight_buf[slot], preferred_element_type=jnp.float32)
-        if k:
-            send_buf[g, k - 1] = part.astype(jnp.bfloat16)
-            part_copy(g, k).start()
-        else:
-            own_part[g] = part
-
-    lax.fori_loop(local_heads // 2, local_heads, own_steps, 0)
+        for g in range(groups):
+            columns = part[:, g * width:(g + 1) * width]
+            if k:
+                send_buf[g, k - 1] = columns.astype(jnp.bfloat16)
+                part_copy(g, k).start()
+            else:
+                own_part[g] = columns
+
     lax.fori_loop(0, pair + 1, fill_bias, 0)
+    lax.fori_loop(local_heads // 4, local_heads // 2, own_steps, 0)
 
     for g in range(groups):
         summed = own_part[g]
@@ -208,11 +210,17 @@
         cache_ref[g] = rounded
         twin_copy(g, 0).start()
 
-        def send(d, _):
+        @pl.when(pair < pairs - 1)
+        def _():
+            direct_copy(g, 1).start()
+
+    def send(d, _):
+        for g in range(groups):
             direct_copy(g, d).start()
-            return 0
-
-        lax.fori_loop(1, pairs - pair, send, 0)
+        return 0
+
+    lax.fori_loop(2, pairs - pair, send, 0)
+    lax.fori_loop(local_heads // 2, local_heads, own_steps, 0)
 
     def attend(s, g, c):
         keys = kv[g, pl.ds(c * CORES, CORES), :, :head_dim].reshape(chunk, head_dim)
@@ -293,6 +301,21 @@
         lax.fori_loop(0, pair + 1, passed, 0)
 
 
+def deliver_kernel(attended, cache, attended_out, cache_out, buf, cache_buf, load_sem, store_sem):
+    steps = attended.shape[0]
+    parts = [(attended.at[s], buf.at[s], attended_out.at[s]) for s in range(steps)]
+    parts.append((cache, cache_buf, cache_out))
+    loads = [pltpu.make_async_copy(p[0], p[1], load_sem.at[i]) for i, p in enumerate(parts)]
+    stores = [pltpu.make_async_copy(p[1], p[2], store_sem.at[i]) for i, p in enumerate(parts)]
+    for load in loads:
+        load.start()
+    for load, store in zip(loads, stores):
+        load.wait()
+        store.start()
+    for store in stores:
+        store.wait()
+
+
 def per_device(sections, shards, features, norm_gain, kv_weight, queries, step_kv, doc_ids, block_lists):
     steps, local_heads, tokens, head_dim = queries.shape
     groups = step_kv.shape[1]
@@ -306,7 +329,7 @@
     dma = pltpu.SemaphoreType.DMA
     vmem = pl.BlockSpec(memory_space=pltpu.VMEM)
     anywhere = pl.BlockSpec(memory_space=pl.ANY)
-    return pl.pallas_call(
+    results = pl.pallas_call(
         functools.partial(fused_kernel, sections, shards, local_width * sections, block_len),
         out_shape=(
             jax.ShapeDtypeStruct(queries.shape, jnp.bfloat16),
@@ -319,7 +342,7 @@
             pltpu.VMEM((1, local_width), jnp.float32),
             pltpu.VMEM(queries.shape, jnp.bfloat16),
             pltpu.VMEM(step_kv.shape, jnp.bfloat16),
-            pltpu.VMEM((groups * sections, local_width, width), jnp.bfloat16),
+            pltpu.VMEM((sections, local_width, groups * width), jnp.bfloat16),
             pltpu.VMEM((tokens, local_width), jnp.bfloat16),
             pltpu.VMEM((groups, tokens, width), jnp.float32),
             pltpu.VMEM((groups, others, tokens, width), jnp.bfloat16),
@@ -331,7 +354,7 @@
             pltpu.VMEM((steps, groups, rows, tokens), jnp.float32),
             pltpu.VMEM((steps, groups, rows, width), jnp.float32),
             dma((4,)),
-            dma((groups * sections,)),
+            dma((sections,)),
             dma((groups, others)),
             dma((groups, others)),
             dma((others,)),
@@ -353,6 +376,16 @@
         doc_ids.reshape(shards, tokens),
         block_lists,
     )
+    return pl.pallas_call(
+        deliver_kernel,
+        out_shape=tuple(jax.ShapeDtypeStruct(r.shape, r.dtype) for r in results),
+        in_specs=[anywhere] * 2,
+        out_specs=(anywhere, anywhere),
+        scratch_shapes=[
+            *(pltpu.VMEM(r.shape, r.dtype) for r in results), dma((steps + 1,)), dma((steps + 1,))
+        ],
+        compiler_params=pltpu.CompilerParams(vmem_limit_bytes=60 * 1024 * 1024),
+    )(*results)
 
 
 def solution(mesh):

time: 42.9 us -> 42.4 us (0.988)
  local copies, waits for them, and re-layouts: 3.42 us -> 0 us
  Pallas kernels: 38.5 us -> 41.5 us
    unnamed x4 -> x0, local copies, waits for them, and re-layouts: 3.42 us -> none
    pallas_call x0 -> x1, Pallas kernels: none -> 2.28 us  [per_device(): pl.pallas_call(deliver_kernel, out_shape=tuple((jax.ShapeDtypeStruct(r.sh...]
    pallas_call x1, Pallas kernels: 38.5 us -> 39.2 us  [per_device(): pl.pallas_call(functools.partial(fused_kernel, sections, shards, local_wi...]
where the time goes in v4:
time: 42.4 us; the launch traced here: 42.1 us
  Pallas kernels  41.5 us (98%)
  between operations  0.64 us (2%)
    pallas_call x1, Pallas kernels, per_device(): pl.pallas_call(functools.partial(fused_kernel, sections, shards, local_wi...  39.2 us
    pallas_call x1, Pallas kernels, per_device(): pl.pallas_call(deliver_kernel, out_shape=tuple((jax.ShapeDtypeStruct(r.sh...  2.28 us

profile of v4, /device:TPU:24, one launch (start us, length us, event | category | flops | bytes accessed | tf_op | source)
XLA Modules:
  0.0 42.1 jit_solution(16975993473749531291)
XLA Ops:
  0.6 39.2 %shard_map.86 = (bf16[3,16,128,128]{3,2,1,0:T(8,128)(2,1)}, bf16[2,128,256]{2,1,0:T(8,128)(2,1)}) custom-call(bf16[128,2048]{1,0:T(8,128)(2,1)} %feat_ref.1, f32[1,2048]{1,0:T(1,128)} %bitcast.2, bf16[2048,2048]{1,0:T(8,128)(2,1)} %weight_ref.1, bf16[3,16,128,128]{3,2,1,0:T(8,128)(2,1)} %query_ref.1, bf16[3,2,128,256]{3,2,1,0:T(8,128)(2,1)} %step_ref.1, ...), custom_call_target="tpu_custom_call" | custom-call | tf_op jit(solution)/shard_map/pallas_call | solution.py:332
  39.8 2.3 %shard_map.87 = (bf16[3,16,128,128]{3,2,1,0:T(8,128)(2,1)}, bf16[2,128,256]{2,1,0:T(8,128)(2,1)}) custom-call(bf16[3,16,128,128]{3,2,1,0:T(8,128)(2,1)} %get-tuple-element.4.attended, bf16[2,128,256]{2,1,0:T(8,128)(2,1)} %get-tuple-element.5.cache), custom_call_target="tpu_custom_call" | custom-call | tf_op jit(solution)/shard_map/pallas_call | solution.py:379

commit v5 on v4

--- a/solution.py
+++ b/solution.py
@@ -29,7 +29,7 @@
     features, gain, queries, step_kv, weight_buf, scaled, own_part, send_buf, recv_buf,
     square_send, square_recv, kv, bias, top, acc,
     load_sem, weight_sem, rs_send, rs_recv, sq_send, sq_recv,
-    direct_send, direct_recv, twin_send, twin_recv,
+    chain_send, chain_recv, twin_send, twin_recv,
 ):
     section = lax.axis_index("section")
     shard = lax.axis_index("seq")
@@ -39,8 +39,8 @@
     entries = list_smem.shape[2]
     chunk = CORES * tokens
     pairs = shards // CORES
-    pair, core = shard // CORES, shard % CORES
-    twin = pair * CORES + 1 - core
+    pair = shard // CORES
+    twin = pair * CORES + 1 - shard % CORES
     scale = math.log2(math.e) / math.sqrt(head_dim)
     order = list(range(sections - 1, -1, -1))
     span = groups * width
@@ -67,9 +67,14 @@
             barrier, inc=1, device_id={"section": flipped(section, k, sections)}, device_id_type=MESH
         )
     pl.semaphore_signal(barrier, inc=1, device_id={"seq": twin}, device_id_type=MESH)
-    for d in range(1, pairs):
-        other = (pair + d) % pairs * CORES + core
-        pl.semaphore_signal(barrier, inc=1, device_id={"seq": other}, device_id_type=MESH)
+
+    @pl.when(pair < pairs - 1)
+    def _():
+        pl.semaphore_signal(barrier, inc=1, device_id={"seq": shard + CORES}, device_id_type=MESH)
+
+    @pl.when(pair > 0)
+    def _():
+        pl.semaphore_signal(barrier, inc=1, device_id={"seq": shard - CORES}, device_id_type=MESH)
 
     feature_load.wait()
     gain_load.wait()
@@ -78,7 +83,7 @@
     square_rows = jnp.transpose(jnp.broadcast_to(squares, (tokens, tokens)))[:8]
     square_send[...] = square_rows
 
-    pl.semaphore_wait(barrier, sections + pairs - 1)
+    pl.semaphore_wait(barrier, sections + jnp.where(pair > 0, 1, 0) + jnp.where(pair < pairs - 1, 1, 0))
 
     def square_copy(k):
         return pltpu.make_async_remote_copy(
@@ -94,19 +99,19 @@
             device_id={"section": flipped(section, k, sections)}, device_id_type=MESH,
         )
 
-    def direct_copy(g, d):
-        place = kv.at[g, shard]
+    def chain_copy(g, hop):
+        place = kv.at[g, shard - CORES * hop]
         return pltpu.make_async_remote_copy(
             src_ref=place, dst_ref=place,
-            send_sem=direct_send.at[g, d], recv_sem=direct_recv.at[g, d],
-            device_id={"seq": shard + CORES * d}, device_id_type=MESH,
-        )
-
-    def direct_arrival(g, d):
-        place = kv.at[g, shard - CORES * d]
+            send_sem=chain_send.at[g, hop], recv_sem=chain_recv.at[g, hop + 1],
+            device_id={"seq": shard + CORES}, device_id_type=MESH,
+        )
+
+    def chain_arrival(g, hop):
+        place = kv.at[g, shard - CORES * hop]
         return pltpu.make_async_remote_copy(
             src_ref=place, dst_ref=place,
-            send_sem=direct_send.at[g, d], recv_sem=direct_recv.at[g, d],
+            send_sem=chain_send.at[g, hop], recv_sem=chain_recv.at[g, hop],
             device_id={"seq": twin}, device_id_type=MESH,
         )
 
@@ -212,14 +217,8 @@
 
         @pl.when(pair < pairs - 1)
         def _():
-            direct_copy(g, 1).start()
-
-    def send(d, _):
-        for g in range(groups):
-            direct_copy(g, d).start()
-        return 0
-
-    lax.fori_loop(2, pairs - pair, send, 0)
+            chain_copy(g, 0).start()
+
     lax.fori_loop(local_heads // 2, local_heads, own_steps, 0)
 
     def attend(s, g, c):
@@ -253,24 +252,35 @@
 
         lax.fori_loop(0, steps, body, 0)
 
+    def pass_on(hop):
+        for g in range(groups):
+            chain_arrival(g, hop).wait_recv()
+
+            @pl.when(pair < pairs - 1)
+            def _():
+                chain_copy(g, hop).start()
+
+            twin_copy(g, hop).start()
+
     for g in range(groups):
         twin_arrival(g, 0).wait_recv()
 
+    @pl.when(pair > 0)
+    def _():
+        pass_on(1)
+
     def hop_body(hop, _):
-        c = pair - hop
         for g in range(groups):
-            over_steps(g, c)
-            if g == 0:
-                @pl.when(hop < pair)
-                def _():
-                    for each in range(groups):
-                        direct_arrival(each, hop + 1).wait_recv()
-                        twin_copy(each, hop + 1).start()
+            over_steps(g, pair - hop)
+
+        @pl.when(hop + 2 <= pair)
+        def _():
+            pass_on(hop + 2)
 
         @pl.when(hop < pair)
         def _():
-            for each in range(groups):
-                twin_arrival(each, hop + 1).wait_recv()
+            for g in range(groups):
+                twin_arrival(g, hop + 1).wait_recv()
 
         return 0
 
@@ -289,15 +299,15 @@
         for k in range(1, sections):
             part_copy(g, k).wait_send()
 
-        def sent(d, _):
-            direct_copy(g, d).wait_send()
-            return 0
-
         def passed(hop, _):
             twin_copy(g, hop).wait_send()
+
+            @pl.when(pair < pairs - 1)
+            def _():
+                chain_copy(g, hop).wait_send()
+
             return 0
 
-        lax.fori_loop(1, pairs - pair, sent, 0)
         lax.fori_loop(0, pair + 1, passed, 0)
 
 

time: 42.4 us -> 40.2 us (0.948)
  Pallas kernels: 41.5 us -> 39.3 us
    pallas_call x1, Pallas kernels: 39.2 us -> 37 us  [per_device(): pl.pallas_call(functools.partial(fused_kernel, sections, shards, local_wi...]
where the time goes in v5:
time: 40.2 us; the launch traced here: 39.9 us
  Pallas kernels  39.3 us (98%)
  between operations  0.64 us (2%)
    pallas_call x1, Pallas kernels, per_device(): pl.pallas_call(functools.partial(fused_kernel, sections, shards, local_wi...  37 us
    pallas_call x1, Pallas kernels, per_device(): pl.pallas_call(deliver_kernel, out_shape=tuple((jax.ShapeDtypeStruct(r.sh...  2.28 us

profile of v5, /device:TPU:24, one launch (start us, length us, event | category | flops | bytes accessed | tf_op | source)
XLA Modules:
  0.0 39.9 jit_solution(11538510958602310859)
XLA Ops:
  0.6 37.0 %shard_map.86 = (bf16[3,16,128,128]{3,2,1,0:T(8,128)(2,1)}, bf16[2,128,256]{2,1,0:T(8,128)(2,1)}) custom-call(bf16[128,2048]{1,0:T(8,128)(2,1)} %feat_ref.1, f32[1,2048]{1,0:T(1,128)} %bitcast.2, bf16[2048,2048]{1,0:T(8,128)(2,1)} %weight_ref.1, bf16[3,16,128,128]{3,2,1,0:T(8,128)(2,1)} %query_ref.1, bf16[3,2,128,256]{3,2,1,0:T(8,128)(2,1)} %step_ref.1, ...), custom_call_target="tpu_custom_call" | custom-call | tf_op jit(solution)/shard_map/pallas_call | solution.py:342
  37.6 2.3 %shard_map.87 = (bf16[3,16,128,128]{3,2,1,0:T(8,128)(2,1)}, bf16[2,128,256]{2,1,0:T(8,128)(2,1)}) custom-call(bf16[3,16,128,128]{3,2,1,0:T(8,128)(2,1)} %get-tuple-element.4.attended, bf16[2,128,256]{2,1,0:T(8,128)(2,1)} %get-tuple-element.5.cache), custom_call_target="tpu_custom_call" | custom-call | tf_op jit(solution)/shard_map/pallas_call | solution.py:389
